TPU v7x, 512 devices: a whole 4x8x8 slice. The times are simulated.
512 devices in a mesh: dp: 32 (over x, z), hid: 16 (over y, core).
Axes of the slice: x: 4, y: 8, z: 8, core: 2. Of those that a mesh axis runs over, the one named last changes fastest.
Arguments:
- inputs: bfloat16 [8192, 8192], P('dp', 'hid'), may hold values from -6 to 6
- out_grad: bfloat16 [8192, 8192], P('dp', 'hid'), may hold values from -6 to 6
- home_block: int32 [64], P('hid'), may hold values from 0 to 1
- blocks_up: bfloat16 [64, 3, 256, 256], P('hid', None, 'dp'), may hold values from -0.21875 to 0.21875
- blocks_down: bfloat16 [64, 3, 256, 256], P('hid', None, 'dp'), may hold values from -0.15625 to 0.15625
- up_left: bfloat16 [8192, 128], P('hid', 'dp'), may hold values from -0.0625 to 0.0625
- up_right: bfloat16 [128, 16384], P('dp', 'hid'), may hold values from -0.5 to 0.5
- down_left: bfloat16 [16384, 128], P('hid', 'dp'), may hold values from -0.046875 to 0.046875
- down_right: bfloat16 [128, 8192], P('dp', 'hid'), may hold values from -0.5 to 0.5
Outputs:
- outputs: bfloat16 [8192, 8192], P('dp', 'hid')
- input_grad: bfloat16 [8192, 8192], P('dp', 'hid')
- grad_blocks_up: bfloat16 [64, 3, 256, 256], P('hid', None, 'dp')
- grad_blocks_down: bfloat16 [64, 3, 256, 256], P('hid', None, 'dp')
- grad_up_left: bfloat16 [8192, 128], P('hid', 'dp')
- grad_up_right: bfloat16 [128, 16384], P('dp', 'hid')
- grad_down_left: bfloat16 [16384, 128], P('hid', 'dp')
- grad_down_right: bfloat16 [128, 8192], P('dp', 'hid')
All inputs are finite; a program needn't handle non-finite values.
Results may differ from a plain program's by a relative error of at most 0.022.
Values may be sent and summed in bfloat16 or wider, within the bound.
A program may use at most 64 MiB of HBM per device.

v0:
```python
import jax
import jax.numpy as jnp
from jax import lax
from jax.sharding import PartitionSpec as P

gelu_coef = 0.7978845608028654
cubic_coef = 0.044715


def from_partner(value, axis, distance):
    mask = 2**distance
    pairs = [(source, source ^ mask) for source in range(lax.axis_size(axis))]
    return lax.ppermute(value, axis, pairs)


def gelu_pair(pre_act):
    tangent = jnp.tanh(gelu_coef * (pre_act + cubic_coef * pre_act * pre_act * pre_act))
    activated = 0.5 * pre_act * (1.0 + tangent)
    derivative = 0.5 * (1.0 + tangent) + 0.5 * pre_act * (1.0 - tangent * tangent) * gelu_coef * (
        1.0 + 3.0 * cubic_coef * pre_act * pre_act
    )
    return (activated, derivative)


def per_device(
    inputs, out_grad, home_block, blocks_up, blocks_down, up_left, up_right, down_left, down_right
):
    single = jnp.float32
    half_type = jnp.bfloat16
    highest = lax.Precision.HIGHEST
    row_count, width_dev = inputs.shape
    hid_blocks, slot_count, shard_rows, blk_size = blocks_up.shape
    level_count = slot_count - 1
    in_blocks = width_dev // blk_size
    hidden_dev = hid_blocks * blk_size
    top_bit = lax.axis_size("hid").bit_length() - 1
    grad_scale = float(lax.axis_size("dp") * row_count) ** (-0.5)
    select = (home_block[:, None] == jnp.arange(in_blocks, dtype=jnp.int32)[None, :]).astype(single)
    full_up, full_down, left_in, right_in, left_out, right_out = (
        lax.all_gather(blocks_up, "dp", axis=2, tiled=True),
        lax.all_gather(blocks_down, "dp", axis=2, tiled=True),
        lax.all_gather(up_left, "dp", axis=1, tiled=True),
        lax.all_gather(up_right, "dp", axis=0, tiled=True),
        lax.all_gather(down_left, "dp", axis=1, tiled=True),
        lax.all_gather(down_right, "dp", axis=0, tiled=True),
    )
    rank_in = lax.psum(jnp.dot(inputs, left_in, preferred_element_type=single), "hid")
    rank_in = rank_in.astype(half_type)
    in_pieces = [inputs]
    grad_pieces = [out_grad]
    for level_idx in range(level_count):
        in_pieces.append(from_partner(inputs, "hid", top_bit - 1 - level_idx))

    def pick_blocks(pieces):
        stacked = jnp.stack(pieces, 0).reshape(slot_count, row_count, in_blocks, blk_size)
        return jnp.take(stacked, home_block, axis=2)

    picked = pick_blocks(in_pieces)
    part_rows = picked
    up_sum = jnp.einsum("sthk,hskn->thn", part_rows, full_up, preferred_element_type=single)
    pre_act = up_sum.reshape(row_count, hidden_dev) + jnp.dot(
        rank_in, right_in, preferred_element_type=single
    )
    activated, derivative = gelu_pair(pre_act)
    hidden = activated.astype(half_type)
    hidden_blocks = hidden.reshape(row_count, hid_blocks, blk_size)
    rank_mid = lax.psum(jnp.dot(hidden, left_out, preferred_element_type=single), "hid").astype(
        half_type
    )
    part_rows = hidden_blocks
    down_sum = jnp.einsum("thk,hskn->sthn", part_rows, full_down, preferred_element_type=single)
    placed = jnp.einsum("sthn,hi->stin", down_sum, select, precision=highest)
    total = placed[0]
    for level_idx in range(level_count):
        arrived = from_partner(placed[level_idx + 1], "hid", top_bit - 1 - level_idx)
        total = total + arrived
    outputs = (
        total.reshape(row_count, width_dev)
        + jnp.dot(rank_mid, right_out, preferred_element_type=single)
    ).astype(half_type)
    rank_back = lax.psum(jnp.dot(out_grad, right_out.T, preferred_element_type=single), "hid")
    rank_back = rank_back.astype(half_type)
    for level_idx in range(level_count):
        grad_pieces.append(from_partner(out_grad, "hid", top_bit - 1 - level_idx))
    grad_picked = pick_blocks(grad_pieces)
    grad_hidden = jnp.einsum(
        "sthn,hskn->thk", grad_picked, full_down, preferred_element_type=single
    )
    grad_pre = (
        (
            grad_hidden.reshape(row_count, hidden_dev)
            + jnp.dot(rank_back, left_out.T, preferred_element_type=single)
        )
        * derivative
    ).astype(half_type)
    rank_grad = lax.psum(
        jnp.dot(grad_pre, right_in.T, preferred_element_type=single), "hid"
    ).astype(half_type)
    grad_blocks = grad_pre.reshape(row_count, hid_blocks, blk_size)
    back_sum = jnp.einsum("thn,hskn->sthk", grad_blocks, full_up, preferred_element_type=single)
    back_placed = jnp.einsum("sthk,hi->stik", back_sum, select, precision=highest)
    back_total = back_placed[0]
    for level_idx in range(level_count):
        arrived = from_partner(back_placed[level_idx + 1], "hid", top_bit - 1 - level_idx)
        back_total = back_total + arrived
    input_grad = (
        back_total.reshape(row_count, width_dev)
        + jnp.dot(rank_grad, left_in.T, preferred_element_type=single)
    ).astype(half_type)
    summed = (
        lax.psum_scatter(
            (
                grad_scale
                * jnp.einsum("sthk,thn->hskn", picked, grad_blocks, preferred_element_type=single)
            ).astype(jnp.bfloat16),
            "dp",
            scatter_dimension=2,
            tiled=True,
        ).astype(jnp.float32),
        lax.psum_scatter(
            (
                grad_scale
                * jnp.einsum(
                    "thk,sthn->hskn", hidden_blocks, grad_picked, preferred_element_type=single
                )
            ).astype(jnp.bfloat16),
            "dp",
            scatter_dimension=2,
            tiled=True,
        ).astype(jnp.float32),
        lax.psum_scatter(
            (grad_scale * jnp.dot(inputs.T, rank_grad, preferred_element_type=single)).astype(
                jnp.bfloat16
            ),
            "dp",
            scatter_dimension=1,
            tiled=True,
        ).astype(jnp.float32),
        lax.psum_scatter(
            (grad_scale * jnp.dot(rank_in.T, grad_pre, preferred_element_type=single)).astype(
                jnp.bfloat16
            ),
            "dp",
            scatter_dimension=0,
            tiled=True,
        ).astype(jnp.float32),
        lax.psum_scatter(
            (grad_scale * jnp.dot(hidden.T, rank_back, preferred_element_type=single)).astype(
                jnp.bfloat16
            ),
            "dp",
            scatter_dimension=1,
            tiled=True,
        ).astype(jnp.float32),
        lax.psum_scatter(
            (grad_scale * jnp.dot(rank_mid.T, out_grad, preferred_element_type=single)).astype(
                jnp.bfloat16
            ),
            "dp",
            scatter_dimension=0,
            tiled=True,
        ).astype(jnp.float32),
    )
    return (outputs, input_grad) + tuple((summed_part.astype(half_type) for summed_part in summed))


def solution(mesh):
    placed = (
        P("dp", "hid"),
        P("dp", "hid"),
        P("hid"),
        P("hid", None, "dp", None),
        P("hid", None, "dp", None),
        P("hid", "dp"),
        P("dp", "hid"),
        P("hid", "dp"),
        P("dp", "hid"),
    )
    return jax.shard_map(
        per_device,
        mesh=mesh,
        in_specs=placed,
        out_specs=(
            P("dp", "hid"),
            P("dp", "hid"),
            P("hid", None, "dp", None),
            P("hid", None, "dp", None),
            P("hid", "dp"),
            P("dp", "hid"),
            P("hid", "dp"),
            P("dp", "hid"),
        ),
        check_vma=False,
    )
```

profile of v0, /device:TPU:8, one launch (start us, length us, event | category | flops | bytes accessed | tf_op | source)
XLA Modules:
  0.0 738.6 jit_solution(1994460682840392459)
XLA Ops:
  8.7 1.1 copy.54
  9.8 6.8 collective-permute-start
  16.7 2.7 collective-permute-start.1
  19.4 1.1 copy.63
  20.5 4.7 collective-permute-start.4
  25.2 2.2 collective-permute-start.5
  27.6 49.3 %all-gather = bf16[32,4,512]{2,1,0:T(4,128)(2,1)S(1)} all-gather(bf16[1,4,512]{2,1,0:T(4,128)(2,1)S(1)} %bitcast.138), channel_id=1, replica_groups=mesh['dp'=32,'hid'=16] {'dp'}, dimensions={0}, use_global_device_ids=true | all-gather | bytes 135168 | tf_op jit(solution)/shard_map/all_gather | solution.py:42
  77.2 42.4 %all-gather.3 = bf16[32,4,512]{2,1,0:T(4,128)(2,1)S(1)} all-gather(bf16[1,4,512]{2,1,0:T(4,128)(2,1)S(1)} %bitcast.139), channel_id=1, replica_groups=mesh['dp'=32,'hid'=16] {'dp'}, dimensions={0}, use_global_device_ids=true | all-gather | bytes 135168 | tf_op jit(solution)/shard_map/all_gather | solution.py:45
  119.9 46.7 %all-gather.1 = bf16[32,4,1024]{2,1,0:T(4,128)(2,1)S(1)} all-gather(bf16[1,4,1024]{2,1,0:T(4,128)(2,1)S(1)} %bitcast.136), channel_id=1, replica_groups=mesh['dp'=32,'hid'=16] {'dp'}, dimensions={0}, use_global_device_ids=true | all-gather | bytes 270336 | tf_op jit(solution)/shard_map/all_gather | solution.py:43
  166.7 0.8 copy.66
  167.6 45.5 %all-reduce.13 = (bf16[256,128]{1,0:T(8,128)(2,1)S(1)}, bf16[256,128]{1,0:T(8,128)(2,1)S(1)}) all-reduce(f32[256,128]{1,0:T(8,128)S(1)} %fusion.57, f32[256,128]{1,0:T(8,128)S(1)} %fusion.59), channel_id=1, replica_groups=mesh['dp'=32,'hid'=16] {'hid'}, use_global_device_ids=true, to_apply=%region_0.2 | all-reduce | flops 65536 | bytes 393216 | tf_op jit(solution)/shard_map/psum | solution.py:47
  213.1 48.1 %all-gather.2 = bf16[32,4,1024]{2,1,0:T(4,128)(2,1)S(1)} all-gather(bf16[1,4,1024]{2,1,0:T(4,128)(2,1)S(1)} %bitcast.137), channel_id=1, replica_groups=mesh['dp'=32,'hid'=16] {'dp'}, dimensions={0}, use_global_device_ids=true | all-gather | bytes 270336 | tf_op jit(solution)/shard_map/all_gather | solution.py:44
  262.3 0.8 copy.67
  263.1 0.8 copy.68
  264.7 1.8 pad_maximum_fusion.1
  266.5 1.9 gather_fusion.1
  268.4 3.2 fusion.8
  271.6 2.6 copy.60
  274.2 3.1 fusion.5
  277.4 2.7 copy.89
  282.5 1.0 fusion.21
  284.1 1.0 fusion.22
  285.1 48.0 %all-reduce.14 = (bf16[256,128]{1,0:T(8,128)(2,1)S(1)}, bf16[256,128]{1,0:T(8,128)(2,1)S(1)}) all-reduce(f32[256,128]{1,0:T(8,128)S(1)} %fusion.58, f32[256,128]{1,0:T(8,128)S(1)} %fusion.60), channel_id=1, replica_groups=mesh['dp'=32,'hid'=16] {'hid'}, use_global_device_ids=true, to_apply=%region_1.0 | all-reduce | flops 65536 | bytes 393216 | tf_op jit(solution)/shard_map/psum | solution.py:67
  333.1 0.9 fusion.24
  334.0 0.9 fusion.25
  334.8 2.3 fusion.10
  337.1 2.4 copy.76
  339.7 1.4 dynamic-slice
  342.8 0.9 multiply_convert_fusion.1
  343.7 1.4 copy.117
  345.0 2.9 reshape.97
  347.9 1.4 copy-done.3
  349.9 4.1 fusion.16
  354.4 7.7 %collective-permute-start.6 = (f32[256,2,256]{2,1,0:T(2,128)S(1)}, f32[256,2,256]{2,1,0:T(2,128)S(1)}, u32[]{:S(2)}, u32[]{:S(2)}) collective-permute-start(f32[256,2,256]{2,1,0:T(2,128)S(1)} %get-tuple-element.50), channel_id=1, source_target_pairs={{0,8},{1,9},{2,10},{3,11},{4,12},{5,13},{6,14},{7,15},{8,0},{9,1},... | collective-permute-start | bytes 1572872 | tf_op jit(solution)/shard_map/ppermute | solution.py:13
  362.1 1.9 collective-permute-start.7
  364.6 4.1 fusion.13
  369.1 7.0 collective-permute-start.2
  376.1 1.9 collective-permute-start.3
  378.4 62.6 %collective-permute-done.7 = f32[256,2,256]{2,1,0:T(2,128)S(1)} collective-permute-done((f32[256,2,256]{2,1,0:T(2,128)S(1)}, f32[256,2,256]{2,1,0:T(2,128)S(1)}, u32[]{:S(2)}, u32[]{:S(2)}) %collective-permute-start.7) | collective-permute-done | bytes 524320 | tf_op jit(solution)/shard_map/ppermute | solution.py:13
  441.4 10.7 %collective-permute-done.3 = f32[256,2,256]{2,1,0:T(2,128)S(1)} collective-permute-done((f32[256,2,256]{2,1,0:T(2,128)S(1)}, f32[256,2,256]{2,1,0:T(2,128)S(1)}, u32[]{:S(2)}, u32[]{:S(2)}) %collective-permute-start.3) | collective-permute-done | bytes 524320 | tf_op jit(solution)/shard_map/ppermute | solution.py:13
  452.5 0.9 add_convert_fusion
  453.5 52.5 %all-reduce.12.cloned.1.call-done = (bf16[4,3,256,256]{3,0,1,2:T(4,128)(2,1)}, bf16[512,128]{0,1:T(8,128)(2,1)}, bf16[128,1024]{1,0:T(8,128)(2,1)}, bf16[1024,128]{0,1:T(8,128)(2,1)}, bf16[128,512]{1,0:T(8,128)(2,1)}) async-done(((bf16[4,3,256,256]{3,0,1,2:T(4,128)(2,1)}, bf16[512,128]{0,1:T(8,128)(2,1)}, bf16[128,1024]{1,0:T(8,128)(2,1)}, bf16[1024,128]{0,1:T(8,128)(2,1)}, bf16[128,512]{1,0:T(8,128)(2,1)}), ...) | async-done | bytes 2359312
  507.4 1.3 constant_dynamic-slice_fusion
  508.7 1.3 constant_dynamic-slice_fusion.3
  510.0 1.3 constant_dynamic-slice_fusion.1
  511.3 1.3 constant_dynamic-slice_fusion.2
  512.6 218.0 %reduce-scatter.4.cloned.1.call-done = bf16[8,3072]{1,0:T(8,128)(2,1)} async-done(((bf16[256,3072]{1,0:T(8,128)(2,1)}), bf16[8,3072]{1,0:T(8,128)(2,1)}) %reduce-scatter.4.cloned.1.call-update) | async-done | bytes 49168
  730.6 0.9 reshape.98
  (78 shorter events, 12.9 us)
Async XLA Ops:
  7.2 69.8 %copy-start.2 = (bf16[256,512]{1,0:T(8,128)(2,1)S(1)}, bf16[256,512]{1,0:T(8,128)(2,1)}, u32[]{:S(2)}) copy-start(bf16[256,512]{1,0:T(8,128)(2,1)} %param.11) | copy-start | bytes 786436
  7.2 112.5 %copy-start.1 = (bf16[256,512]{1,0:T(8,128)(2,1)S(1)}, bf16[256,512]{1,0:T(8,128)(2,1)}, u32[]{:S(2)}) copy-start(bf16[256,512]{1,0:T(8,128)(2,1)} %param.12) | copy-start | bytes 786436
  7.2 20.4 %copy-start.12 = (bf16[512,4]{0,1:T(4,128)(2,1)S(1)}, bf16[512,4]{0,1:T(4,128)(2,1)}, u32[]{:S(2)}) copy-start(bf16[512,4]{0,1:T(4,128)(2,1)} %param.16) | copy-start | bytes 12292
  7.2 70.0 %copy-start.13 = (bf16[4,512]{1,0:T(4,128)(2,1)S(1)}, bf16[4,512]{1,0:T(4,128)(2,1)}, u32[]{:S(2)}) copy-start(bf16[4,512]{1,0:T(4,128)(2,1)} %param.19) | copy-start | bytes 12292
  7.2 261.2 %all-gather.7.cloned.1.call-start = ((), (), s32[]{:S(2)}) async-start(), calls=%async_computation.1 | async-start | bytes 1622016 | tf_op jit(solution)/shard_map/all_gather | solution.py:40
  7.9 266.3 %all-gather.9.cloned.1.call-start = ((), (), s32[]{:S(2)}) async-start(), calls=%async_computation.2 | async-start | bytes 1622016 | tf_op jit(solution)/shard_map/all_gather | solution.py:41
  8.7 497.2 %all-reduce.12.cloned.1.call-start = ((), (), s32[]{:S(2)}) async-start(), calls=%async_computation.4 | async-start | bytes 4718592
  9.8 110.1 %copy-start.10 = (bf16[4,1024]{1,0:T(4,128)(2,1)S(1)}, bf16[4,1024]{1,0:T(4,128)(2,1)}, u32[]{:S(2)}) copy-start(bf16[4,1024]{1,0:T(4,128)(2,1)} %param.17) | copy-start | bytes 24580
  9.8 252.2 %collective-permute-start = (bf16[256,512]{0,1:T(8,128)(2,1)S(1)}, bf16[256,512]{0,1:T(8,128)(2,1)S(1)}, u32[]{:S(2)}, u32[]{:S(2)}) collective-permute-start(bf16[256,512]{0,1:T(8,128)(2,1)S(1)} %copy.54), channel_id=1, source_target_pairs={{0,8},{1,9},{2,10},{3,11},{4,12},{5,13},{6,14},{7,15},{8,0},{9,1},... | collective-permute-start | bytes 786440 | tf_op jit(solution)/shard_map/ppermute | solution.py:13
  16.7 245.5 %collective-permute-start.1 = (bf16[256,512]{0,1:T(8,128)(2,1)S(1)}, bf16[256,512]{0,1:T(8,128)(2,1)S(1)}, u32[]{:S(2)}, u32[]{:S(2)}) collective-permute-start(bf16[256,512]{0,1:T(8,128)(2,1)S(1)} %copy.54), channel_id=1, source_target_pairs={{0,4},{1,5},{2,6},{3,7},{4,0},{5,1},{6,2},{7,3},{8,12},{9,13},{10,... | collective-permute-start | bytes 786440 | tf_op jit(solution)/shard_map/ppermute | solution.py:13
  20.5 241.8 %collective-permute-start.4 = (bf16[256,512]{0,1:T(8,128)(2,1)S(1)}, bf16[256,512]{0,1:T(8,128)(2,1)S(1)}, u32[]{:S(2)}, u32[]{:S(2)}) collective-permute-start(bf16[256,512]{0,1:T(8,128)(2,1)S(1)} %copy.63), channel_id=1, source_target_pairs={{0,8},{1,9},{2,10},{3,11},{4,12},{5,13},{6,14},{7,15},{8,0},{9,1},... | collective-permute-start | bytes 786440 | tf_op jit(solution)/shard_map/ppermute | solution.py:13
  25.2 237.9 %collective-permute-start.5 = (bf16[256,512]{0,1:T(8,128)(2,1)S(1)}, bf16[256,512]{0,1:T(8,128)(2,1)S(1)}, u32[]{:S(2)}, u32[]{:S(2)}) collective-permute-start(bf16[256,512]{0,1:T(8,128)(2,1)S(1)} %copy.63), channel_id=1, source_target_pairs={{0,4},{1,5},{2,6},{3,7},{4,0},{5,1},{6,2},{7,3},{8,12},{9,13},{10,... | collective-permute-start | bytes 786440 | tf_op jit(solution)/shard_map/ppermute | solution.py:13
  27.6 139.9 %copy-start.14 = (s32[4]{0:T(128)S(1)}, s32[4]{0:T(128)}, u32[]{:S(2)}) copy-start(s32[4]{0:T(128)} %param.13) | copy-start | bytes 52
  77.0 136.1 %copy-start.11 = (bf16[1024,4]{0,1:T(4,128)(2,1)S(1)}, bf16[1024,4]{0,1:T(4,128)(2,1)}, u32[]{:S(2)}) copy-start(bf16[1024,4]{0,1:T(4,128)(2,1)} %param.18) | copy-start | bytes 24580
  264.7 3.6 copy-start.4
  271.6 2.7 copy-start.6
  277.4 2.7 copy-start.8
  280.1 0.9 copy-start.7
  280.1 1.3 copy-start.9
  339.5 3.3 copy-start.5
  339.5 391.1 %reduce-scatter.4.cloned.1.call-start = ((), (), s32[]{:S(2)}) async-start(), calls=%async_computation.3 | async-start | bytes 1622016
  347.9 1.4 copy-start.3
  354.0 10.0 %copy-start = (bf16[4,3,256,256]{3,2,1,0:T(8,128)(2,1)S(1)}, bf16[4,3,256,256]{3,2,1,0:T(8,128)(2,1)}, u32[]{:S(2)}) copy-start(bf16[4,3,256,256]{3,2,1,0:T(8,128)(2,1)} %all-gather.9.cloned.1.call-done) | copy-start | bytes 4718596
  354.4 24.0 %collective-permute-start.6 = (f32[256,2,256]{2,1,0:T(2,128)S(1)}, f32[256,2,256]{2,1,0:T(2,128)S(1)}, u32[]{:S(2)}, u32[]{:S(2)}) collective-permute-start(f32[256,2,256]{2,1,0:T(2,128)S(1)} %get-tuple-element.50), channel_id=1, source_target_pairs={{0,8},{1,9},{2,10},{3,11},{4,12},{5,13},{6,14},{7,15},{8,0},{9,1},... | collective-permute-start | bytes 1572872 | tf_op jit(solution)/shard_map/ppermute | solution.py:13
  362.1 78.9 %collective-permute-start.7 = (f32[256,2,256]{2,1,0:T(2,128)S(1)}, f32[256,2,256]{2,1,0:T(2,128)S(1)}, u32[]{:S(2)}, u32[]{:S(2)}) collective-permute-start(f32[256,2,256]{2,1,0:T(2,128)S(1)} %get-tuple-element.51), channel_id=1, source_target_pairs={{0,4},{1,5},{2,6},{3,7},{4,0},{5,1},{6,2},{7,3},{8,12},{9,13},{10,... | collective-permute-start | bytes 1572872 | tf_op jit(solution)/shard_map/ppermute | solution.py:13
  369.1 72.3 %collective-permute-start.2 = (f32[256,2,256]{2,1,0:T(2,128)S(1)}, f32[256,2,256]{2,1,0:T(2,128)S(1)}, u32[]{:S(2)}, u32[]{:S(2)}) collective-permute-start(f32[256,2,256]{2,1,0:T(2,128)S(1)} %get-tuple-element.52), channel_id=1, source_target_pairs={{0,8},{1,9},{2,10},{3,11},{4,12},{5,13},{6,14},{7,15},{8,0},{9,1},... | collective-permute-start | bytes 1572872 | tf_op jit(solution)/shard_map/ppermute | solution.py:13
  376.1 76.1 %collective-permute-start.3 = (f32[256,2,256]{2,1,0:T(2,128)S(1)}, f32[256,2,256]{2,1,0:T(2,128)S(1)}, u32[]{:S(2)}, u32[]{:S(2)}) collective-permute-start(f32[256,2,256]{2,1,0:T(2,128)S(1)} %get-tuple-element.53), channel_id=1, source_target_pairs={{0,4},{1,5},{2,6},{3,7},{4,0},{5,1},{6,2},{7,3},{8,12},{9,13},{10,... | collective-permute-start | bytes 1572872 | tf_op jit(solution)/shard_map/ppermute | solution.py:13
Sparse Core Ops, SparseCore 0:
  11.1 83.7 all-gather.6
  97.9 77.6 all-gather.8
  339.6 166.2 all-reduce.11
  510.8 219.7 reduce-scatter.3
where the time goes:
time: 740 us; the launch traced here: 739 us
  waiting for transfers between devices  345 us (47%)
  blocking collectives  280 us (38%)
  starting transfers between devices  35.3 us (5%)
  local copies, waits for them, and re-layouts  33.8 us (5%)
  matrix products  25.2 us (3%)
  between operations  15.6 us (2%)
    unnamed x6, waiting for transfers between devices  272 us
    ppermute x8, waiting for transfers between devices, from_partner(): return lax.ppermute(value, axis, pairs)  73.3 us
    all_gather x1, blocking collectives, per_device(): lax.all_gather(up_left, 'dp', axis=1, tiled=True)  49.3 us
    all_gather x1, blocking collectives, per_device(): lax.all_gather(down_left, 'dp', axis=1, tiled=True)  48.1 us
    psum x1, blocking collectives, per_device(): lax.psum(jnp.dot(hidden, left_out, preferred_element_type=single), 'hid')  48 us
    all_gather x1, blocking collectives, per_device(): lax.all_gather(up_right, 'dp', axis=0, tiled=True)  46.7 us
    psum x1, blocking collectives, per_device(): lax.psum(jnp.dot(inputs, left_in, preferred_element_type=single), 'hid')  45.5 us
    all_gather x1, blocking collectives, per_device(): lax.all_gather(down_right, 'dp', axis=0, tiled=True)  42.4 us
  transfers between devices with their start and end apart: 12, of which 4 were waited for; matrix products, arithmetic and copies ran while one was open for 6% of the time, Pallas kernels for 0%

commit v1 on v0

--- a/solution.py
+++ b/solution.py
@@ -36,11 +36,28 @@
     top_bit = lax.axis_size("hid").bit_length() - 1
     grad_scale = float(lax.axis_size("dp") * row_count) ** (-0.5)
     select = (home_block[:, None] == jnp.arange(in_blocks, dtype=jnp.int32)[None, :]).astype(single)
+
+    def produce_core(u_in):
+        f_next, current_arr = (lax.axis_size("dp"), lax.axis_index("dp"))
+        later, outcome_arr = (u_in, 1)
+        while outcome_arr < f_next:
+            vals = []
+            c = 0
+            while c < f_next:
+                vals.append((c, c ^ outcome_arr))
+                c = c + 1
+            x_now = lax.ppermute(later, "dp", vals)
+            kept_arr = jnp.concatenate([later, x_now], 0)
+            z1 = jnp.concatenate([x_now, later], 0)
+            later = jnp.where(current_arr & outcome_arr == 0, kept_arr, z1)
+            outcome_arr = 2 * outcome_arr
+        return later
+
     full_up, full_down, left_in, right_in, left_out, right_out = (
         lax.all_gather(blocks_up, "dp", axis=2, tiled=True),
         lax.all_gather(blocks_down, "dp", axis=2, tiled=True),
         lax.all_gather(up_left, "dp", axis=1, tiled=True),
-        lax.all_gather(up_right, "dp", axis=0, tiled=True),
+        produce_core(up_right),
         lax.all_gather(down_left, "dp", axis=1, tiled=True),
         lax.all_gather(down_right, "dp", axis=0, tiled=True),
     )

time: 740 us -> 716 us (0.968)
  blocking collectives: 280 us -> 233 us
  starting transfers between devices: 35.3 us -> 53.1 us
    all_gather x1 -> x0, blocking collectives: 46.7 us -> none  [per_device(): lax.all_gather(up_right, 'dp', axis=0, tiled=True)]
    ppermute x0 -> x5, starting transfers between devices: none -> 18 us  [produce_core(): x_now = lax.ppermute(later, 'dp', vals)]
    unnamed x49 -> x42, local copies, waits for them, and re-layouts: 19.2 us -> 17.8 us
  transfers between devices with their start and end apart: 12 -> 17, of which waited for: 4 -> 5; matrix products, arithmetic and copies ran while one was open for 6% -> 7% of each run, Pallas kernels for 0% -> 0%
where the time goes in v1:
time: 716 us; the launch traced here: 715 us
  waiting for transfers between devices  349 us (49%)
  blocking collectives  233 us (33%)
  starting transfers between devices  53.1 us (7%)
  local copies, waits for them, and re-layouts  31.1 us (4%)
  matrix products  29.9 us (4%)
  between operations  15.6 us (2%)
    unnamed x6, waiting for transfers between devices  273 us
    ppermute x8, waiting for transfers between devices, from_partner(): return lax.ppermute(value, axis, pairs)  73.1 us
    all_gather x1, blocking collectives, per_device(): lax.all_gather(down_left, 'dp', axis=1, tiled=True)  48.4 us
    all_gather x1, blocking collectives, per_device(): lax.all_gather(up_left, 'dp', axis=1, tiled=True)  48.2 us
    psum x1, blocking collectives, per_device(): lax.psum(jnp.dot(hidden, left_out, preferred_element_type=single), 'hid')  48 us
    psum x1, blocking collectives, per_device(): lax.psum(jnp.dot(inputs, left_in, preferred_element_type=single), 'hid')  46.7 us
    all_gather x1, blocking collectives, per_device(): lax.all_gather(down_right, 'dp', axis=0, tiled=True)  41.7 us
    ppermute x8, starting transfers between devices, from_partner(): return lax.ppermute(value, axis, pairs)  34.8 us
  transfers between devices with their start and end apart: 17, of which 5 were waited for; matrix products, arithmetic and copies ran while one was open for 7% of the time, Pallas kernels for 0%

profile of v1, /device:TPU:8, one launch (start us, length us, event | category | flops | bytes accessed | tf_op | source)
XLA Modules:
  0.0 715.1 jit_solution(6504140945987221768)
XLA Ops:
  8.7 1.1 copy.54
  9.8 6.8 collective-permute-start
  16.7 2.7 collective-permute-start.1
  19.4 1.1 copy.63
  20.5 4.7 collective-permute-start.9
  25.2 2.2 collective-permute-start.10
  27.4 4.3 collective-permute-start.2
  31.7 48.2 %all-gather = bf16[32,4,512]{2,1,0:T(4,128)(2,1)S(1)} all-gather(bf16[1,4,512]{2,1,0:T(4,128)(2,1)} %bitcast.134), channel_id=1, replica_groups=mesh['dp'=32,'hid'=16] {'dp'}, dimensions={0}, use_global_device_ids=true | all-gather | bytes 135168 | tf_op jit(solution)/shard_map/all_gather | solution.py:59
  80.0 41.7 %all-gather.2 = bf16[32,4,512]{2,1,0:T(4,128)(2,1)S(1)} all-gather(bf16[1,4,512]{2,1,0:T(4,128)(2,1)} %bitcast.135), channel_id=1, replica_groups=mesh['dp'=32,'hid'=16] {'dp'}, dimensions={0}, use_global_device_ids=true | all-gather | bytes 135168 | tf_op jit(solution)/shard_map/all_gather | solution.py:62
  122.3 2.2 collective-permute-start.3
  124.4 46.7 %all-reduce.13 = (bf16[256,128]{1,0:T(8,128)(2,1)}, bf16[256,128]{1,0:T(8,128)(2,1)}) all-reduce(f32[256,128]{1,0:T(8,128)S(1)} %fusion.60, f32[256,128]{1,0:T(8,128)S(1)} %fusion.62), channel_id=1, replica_groups=mesh['dp'=32,'hid'=16] {'hid'}, use_global_device_ids=true, to_apply=%region_0.2 | all-reduce | flops 65536 | bytes 393216 | tf_op jit(solution)/shard_map/psum | solution.py:64
  172.1 5.0 collective-permute-start.4
  177.1 48.4 %all-gather.1 = bf16[32,4,1024]{2,1,0:T(4,128)(2,1)S(1)} all-gather(bf16[1,4,1024]{2,1,0:T(4,128)(2,1)S(1)} %bitcast.133), channel_id=1, replica_groups=mesh['dp'=32,'hid'=16] {'dp'}, dimensions={0}, use_global_device_ids=true | all-gather | bytes 270336 | tf_op jit(solution)/shard_map/all_gather | solution.py:61
  225.6 3.0 collective-permute-start.5
  228.5 3.2 collective-permute-done.5
  231.7 3.6 collective-permute-start.6
  238.1 1.8 pad_maximum_fusion.1
  239.9 1.9 gather_fusion.1
  241.8 3.1 fusion.8
  244.9 3.7 fusion.5
  248.5 1.6 copy.60
  250.1 2.5 copy.89
  252.6 2.6 multiply_convert_fusion.2
  256.1 1.0 fusion.22
  257.0 2.0 fusion.20
  259.0 1.0 fusion.21
  260.0 1.3 fusion.39
  261.3 48.0 %all-reduce.14 = (bf16[256,128]{1,0:T(8,128)(2,1)S(1)}, bf16[256,128]{1,0:T(8,128)(2,1)S(1)}) all-reduce(f32[256,128]{1,0:T(8,128)S(1)} %fusion.61, f32[256,128]{1,0:T(8,128)S(1)} %fusion.39), channel_id=1, replica_groups=mesh['dp'=32,'hid'=16] {'hid'}, use_global_device_ids=true, to_apply=%region_1.3 | all-reduce | flops 65536 | bytes 393216 | tf_op jit(solution)/shard_map/psum | solution.py:84
  311.0 2.3 fusion.10
  313.3 2.3 copy.76
  315.9 1.4 dynamic-slice
  319.8 1.4 copy.117
  321.2 2.9 reshape.95
  324.1 1.4 copy-done
  326.1 4.1 fusion.13
  330.5 7.5 %collective-permute-start.7 = (f32[256,2,256]{2,1,0:T(2,128)S(1)}, f32[256,2,256]{2,1,0:T(2,128)S(1)}, u32[]{:S(2)}, u32[]{:S(2)}) collective-permute-start(f32[256,2,256]{2,1,0:T(2,128)S(1)} %get-tuple-element.52), channel_id=1, source_target_pairs={{0,8},{1,9},{2,10},{3,11},{4,12},{5,13},{6,14},{7,15},{8,0},{9,1},... | collective-permute-start | bytes 1572872 | tf_op jit(solution)/shard_map/ppermute | solution.py:13
  338.0 1.9 collective-permute-start.8
  340.6 4.1 fusion.16
  345.0 7.0 collective-permute-start.11
  352.0 1.9 collective-permute-start.12
  354.4 62.4 %collective-permute-done.8 = f32[256,2,256]{2,1,0:T(2,128)S(1)} collective-permute-done((f32[256,2,256]{2,1,0:T(2,128)S(1)}, f32[256,2,256]{2,1,0:T(2,128)S(1)}, u32[]{:S(2)}, u32[]{:S(2)}) %collective-permute-start.8) | collective-permute-done | bytes 524320 | tf_op jit(solution)/shard_map/ppermute | solution.py:13
  417.2 10.7 %collective-permute-done.12 = f32[256,2,256]{2,1,0:T(2,128)S(1)} collective-permute-done((f32[256,2,256]{2,1,0:T(2,128)S(1)}, f32[256,2,256]{2,1,0:T(2,128)S(1)}, u32[]{:S(2)}, u32[]{:S(2)}) %collective-permute-start.12) | collective-permute-done | bytes 524320 | tf_op jit(solution)/shard_map/ppermute | solution.py:13
  429.3 53.1 %all-reduce.12.cloned.1.call-done = (bf16[4,3,256,256]{3,0,1,2:T(4,128)(2,1)}, bf16[512,128]{0,1:T(8,128)(2,1)}, bf16[128,1024]{1,0:T(8,128)(2,1)}, bf16[1024,128]{0,1:T(8,128)(2,1)}, bf16[128,512]{1,0:T(8,128)(2,1)}) async-done(((bf16[4,3,256,256]{3,0,1,2:T(4,128)(2,1)}, bf16[512,128]{0,1:T(8,128)(2,1)}, bf16[128,1024]{1,0:T(8,128)(2,1)}, bf16[1024,128]{0,1:T(8,128)(2,1)}, bf16[128,512]{1,0:T(8,128)(2,1)}), ...) | async-done | bytes 2359312
  483.9 1.3 constant_dynamic-slice_fusion
  485.2 1.3 constant_dynamic-slice_fusion.3
  486.5 1.3 constant_dynamic-slice_fusion.1
  487.8 1.3 constant_dynamic-slice_fusion.2
  489.1 218.0 %reduce-scatter.4.cloned.1.call-done = bf16[8,3072]{1,0:T(8,128)(2,1)} async-done(((bf16[256,3072]{1,0:T(8,128)(2,1)}), bf16[8,3072]{1,0:T(8,128)(2,1)}) %reduce-scatter.4.cloned.1.call-update) | async-done | bytes 49168
  (84 shorter events, 17.0 us)
Async XLA Ops:
  7.2 114.6 %copy-start.2 = (bf16[256,512]{1,0:T(8,128)(2,1)S(1)}, bf16[256,512]{1,0:T(8,128)(2,1)}, u32[]{:S(2)}) copy-start(bf16[256,512]{1,0:T(8,128)(2,1)} %param.11) | copy-start | bytes 786436
  7.2 114.8 %copy-start.1 = (bf16[256,512]{1,0:T(8,128)(2,1)S(1)}, bf16[256,512]{1,0:T(8,128)(2,1)}, u32[]{:S(2)}) copy-start(bf16[256,512]{1,0:T(8,128)(2,1)} %param.12) | copy-start | bytes 786436
  7.2 115.0 %copy-start.9 = (bf16[4,1024]{1,0:T(4,128)(2,1)S(1)}, bf16[4,1024]{1,0:T(4,128)(2,1)}, u32[]{:S(2)}) copy-start(bf16[4,1024]{1,0:T(4,128)(2,1)} %param.17) | copy-start | bytes 24580
  7.2 114.5 %copy-start.10 = (s32[4]{0:T(128)S(1)}, s32[4]{0:T(128)}, u32[]{:S(2)}) copy-start(s32[4]{0:T(128)} %param.13) | copy-start | bytes 52
  7.2 234.5 %all-gather.6.cloned.1.call-start = ((), (), s32[]{:S(2)}) async-start(), calls=%async_computation.1 | async-start | bytes 1622016 | tf_op jit(solution)/shard_map/all_gather | solution.py:57
  7.9 236.9 %all-gather.8.cloned.1.call-start = ((), (), s32[]{:S(2)}) async-start(), calls=%async_computation.2 | async-start | bytes 1622016 | tf_op jit(solution)/shard_map/all_gather | solution.py:58
  8.7 473.7 %all-reduce.12.cloned.1.call-start = ((), (), s32[]{:S(2)}) async-start(), calls=%async_computation.4 | async-start | bytes 4718592
  9.8 225.5 %collective-permute-start = (bf16[256,512]{0,1:T(8,128)(2,1)S(1)}, bf16[256,512]{0,1:T(8,128)(2,1)S(1)}, u32[]{:S(2)}, u32[]{:S(2)}) collective-permute-start(bf16[256,512]{0,1:T(8,128)(2,1)S(1)} %copy.54), channel_id=1, source_target_pairs={{0,8},{1,9},{2,10},{3,11},{4,12},{5,13},{6,14},{7,15},{8,0},{9,1},... | collective-permute-start | bytes 786440 | tf_op jit(solution)/shard_map/ppermute | solution.py:13
  16.7 218.8 %collective-permute-start.1 = (bf16[256,512]{0,1:T(8,128)(2,1)S(1)}, bf16[256,512]{0,1:T(8,128)(2,1)S(1)}, u32[]{:S(2)}, u32[]{:S(2)}) collective-permute-start(bf16[256,512]{0,1:T(8,128)(2,1)S(1)} %copy.54), channel_id=1, source_target_pairs={{0,4},{1,5},{2,6},{3,7},{4,0},{5,1},{6,2},{7,3},{8,12},{9,13},{10,... | collective-permute-start | bytes 786440 | tf_op jit(solution)/shard_map/ppermute | solution.py:13
  20.5 215.2 %collective-permute-start.9 = (bf16[256,512]{0,1:T(8,128)(2,1)S(1)}, bf16[256,512]{0,1:T(8,128)(2,1)S(1)}, u32[]{:S(2)}, u32[]{:S(2)}) collective-permute-start(bf16[256,512]{0,1:T(8,128)(2,1)S(1)} %copy.63), channel_id=1, source_target_pairs={{0,8},{1,9},{2,10},{3,11},{4,12},{5,13},{6,14},{7,15},{8,0},{9,1},... | collective-permute-start | bytes 786440 | tf_op jit(solution)/shard_map/ppermute | solution.py:13
  25.2 211.3 %collective-permute-start.10 = (bf16[256,512]{0,1:T(8,128)(2,1)S(1)}, bf16[256,512]{0,1:T(8,128)(2,1)S(1)}, u32[]{:S(2)}, u32[]{:S(2)}) collective-permute-start(bf16[256,512]{0,1:T(8,128)(2,1)S(1)} %copy.63), channel_id=1, source_target_pairs={{0,4},{1,5},{2,6},{3,7},{4,0},{5,1},{6,2},{7,3},{8,12},{9,13},{10,... | collective-permute-start | bytes 786440 | tf_op jit(solution)/shard_map/ppermute | solution.py:13
  27.4 94.8 %collective-permute-start.2 = (bf16[4,1024]{1,0:T(4,128)(2,1)}, bf16[4,1024]{1,0:T(4,128)(2,1)S(1)}, u32[]{:S(2)}, u32[]{:S(2)}) collective-permute-start(bf16[4,1024]{1,0:T(4,128)(2,1)} %param.17), channel_id=1, source_target_pairs={{0,16},{16,0},{32,48},{48,32},{64,80},{80,64},{96,112},{112,96},{1... | collective-permute-start | bytes 24584 | tf_op jit(solution)/shard_map/ppermute | solution.py:49
  79.9 97.1 %copy-start.8 = (bf16[1024,4]{0,1:T(4,128)(2,1)S(1)}, bf16[1024,4]{0,1:T(4,128)(2,1)}, u32[]{:S(2)}) copy-start(bf16[1024,4]{0,1:T(4,128)(2,1)} %param.18) | copy-start | bytes 24580
  122.3 49.8 %collective-permute-start.3 = (bf16[8,1024]{1,0:T(8,128)(2,1)S(1)}, bf16[8,1024]{1,0:T(8,128)(2,1)S(1)}, u32[]{:S(2)}, u32[]{:S(2)}) collective-permute-start(bf16[8,1024]{1,0:T(8,128)(2,1)S(1)} %maximum_select_fusion.6), channel_id=1, source_target_pairs={{0,32},{16,48},{32,0},{48,16},{64,96},{80,112},{96,64},{112,80},{1... | collective-permute-start | bytes 49160 | tf_op jit(solution)/shard_map/ppermute | solution.py:49
  172.1 53.4 %collective-permute-start.4 = (bf16[16,1024]{1,0:T(8,128)(2,1)S(1)}, bf16[16,1024]{1,0:T(8,128)(2,1)S(1)}, u32[]{:S(2)}, u32[]{:S(2)}) collective-permute-start(bf16[16,1024]{1,0:T(8,128)(2,1)S(1)} %maximum_select_fusion.5), channel_id=1, source_target_pairs={{0,64},{16,80},{32,96},{48,112},{64,0},{80,16},{96,32},{112,48},{1... | collective-permute-start | bytes 98312 | tf_op jit(solution)/shard_map/ppermute | solution.py:49
  225.6 6.2 collective-permute-start.5
  231.7 20.9 %collective-permute-start.6 = (bf16[64,1024]{1,0:T(8,128)(2,1)S(1)}, bf16[64,1024]{1,0:T(8,128)(2,1)}, u32[]{:S(2)}, u32[]{:S(2)}) collective-permute-start(bf16[64,1024]{1,0:T(8,128)(2,1)S(1)} %maximum_select_fusion.1), channel_id=1, source_target_pairs={{0,256},{16,272},{32,288},{48,304},{64,320},{80,336},{96,352},{112... | collective-permute-start | bytes 393224 | tf_op jit(solution)/shard_map/ppermute | solution.py:49
  238.1 3.6 copy-start.4
  250.1 2.6 copy-start.6
  255.2 0.8 copy-start.7
  255.6 1.5 copy-start.11
  315.6 3.3 copy-start.5
  315.7 391.4 %reduce-scatter.4.cloned.1.call-start = ((), (), s32[]{:S(2)}) async-start(), calls=%async_computation.3 | async-start | bytes 1622016
  324.1 1.4 copy-start
  330.2 9.8 %copy-start.3 = (bf16[4,3,256,256]{3,2,1,0:T(8,128)(2,1)S(1)}, bf16[4,3,256,256]{3,2,1,0:T(8,128)(2,1)}, u32[]{:S(2)}) copy-start(bf16[4,3,256,256]{3,2,1,0:T(8,128)(2,1)} %all-gather.6.cloned.1.call-done) | copy-start | bytes 4718596
  330.5 23.8 %collective-permute-start.7 = (f32[256,2,256]{2,1,0:T(2,128)S(1)}, f32[256,2,256]{2,1,0:T(2,128)S(1)}, u32[]{:S(2)}, u32[]{:S(2)}) collective-permute-start(f32[256,2,256]{2,1,0:T(2,128)S(1)} %get-tuple-element.52), channel_id=1, source_target_pairs={{0,8},{1,9},{2,10},{3,11},{4,12},{5,13},{6,14},{7,15},{8,0},{9,1},... | collective-permute-start | bytes 1572872 | tf_op jit(solution)/shard_map/ppermute | solution.py:13
  338.0 78.8 %collective-permute-start.8 = (f32[256,2,256]{2,1,0:T(2,128)S(1)}, f32[256,2,256]{2,1,0:T(2,128)S(1)}, u32[]{:S(2)}, u32[]{:S(2)}) collective-permute-start(f32[256,2,256]{2,1,0:T(2,128)S(1)} %get-tuple-element.53), channel_id=1, source_target_pairs={{0,4},{1,5},{2,6},{3,7},{4,0},{5,1},{6,2},{7,3},{8,12},{9,13},{10,... | collective-permute-start | bytes 1572872 | tf_op jit(solution)/shard_map/ppermute | solution.py:13
  345.0 72.2 %collective-permute-start.11 = (f32[256,2,256]{2,1,0:T(2,128)S(1)}, f32[256,2,256]{2,1,0:T(2,128)S(1)}, u32[]{:S(2)}, u32[]{:S(2)}) collective-permute-start(f32[256,2,256]{2,1,0:T(2,128)S(1)} %get-tuple-element.50), channel_id=1, source_target_pairs={{0,8},{1,9},{2,10},{3,11},{4,12},{5,13},{6,14},{7,15},{8,0},{9,1},... | collective-permute-start | bytes 1572872 | tf_op jit(solution)/shard_map/ppermute | solution.py:13
  352.0 75.9 %collective-permute-start.12 = (f32[256,2,256]{2,1,0:T(2,128)S(1)}, f32[256,2,256]{2,1,0:T(2,128)S(1)}, u32[]{:S(2)}, u32[]{:S(2)}) collective-permute-start(f32[256,2,256]{2,1,0:T(2,128)S(1)} %get-tuple-element.51), channel_id=1, source_target_pairs={{0,4},{1,5},{2,6},{3,7},{4,0},{5,1},{6,2},{7,3},{8,12},{9,13},{10,... | collective-permute-start | bytes 1572872 | tf_op jit(solution)/shard_map/ppermute | solution.py:13
Sparse Core Ops, SparseCore 0:
  11.1 83.8 all-gather.5
  98.0 77.4 all-gather.7
  315.8 166.6 all-reduce.11
  487.3 219.7 reduce-scatter.3
